TPU v7x, 32 devices: a whole 2x2x4 slice. The times are simulated.
32 devices in a mesh: feat: 8 (over y, x, core), rows: 4 (over z).
Axes of the slice: x: 2, y: 2, z: 4, core: 2. Of those that a mesh axis runs over, the one named last changes fastest.
Arguments:
- binned: int32 [8192, 512], P('rows', 'feat'), may hold values from 0 to 255
- node_of: int32 [8192], P('rows'), may hold values from 0 to 31
- margin: float32 [8192], P('rows'), may hold values from -6 to 6
- labels: float32 [8192], P('rows'), may hold values from 0 to 1
- split_feature: int32 [32], replicated, may hold values from 0 to 511
- split_bin: int32 [32], replicated, may hold values from 0 to 255
Outputs:
- histogram: float32 [32, 2, 512, 256], P('rows', None, 'feat')
- margin_out: float32 [8192], P('rows')
- child_out: int32 [8192], P('rows')
- grad_out: float32 [2, 8192], P(None, 'rows')
All inputs are finite; a program needn't handle non-finite values.
Results may differ from a plain program's by a relative error of at most 0.0045.
Values may be sent and summed in bfloat16 or wider, within the bound.
A program may use at most 64 MiB of HBM per device.

v0:
```python
import jax
import jax.numpy as jnp
from jax import lax
from jax.sharding import PartitionSpec as P

BINS = 256


def leaf_table(selected, split_rows):
    below = (jnp.arange(selected.shape[2])[None, :] <= split_rows[:, None]).astype(jnp.float32)
    left = jnp.sum(selected * below[:, None, :], axis=2)
    whole = jnp.sum(selected, axis=2)
    return jnp.concatenate([left, whole], axis=1)


def node_sums(nodes_here, feature_ids, split_rows, feat_start):
    feat_count = nodes_here.shape[2]
    local = feature_ids - feat_start
    owned = (local >= 0) & (local < feat_count)
    chooser = ((local[:, None] == jnp.arange(feat_count)[None, :]) & owned[:, None]).astype(
        jnp.float32
    )
    selected = jnp.einsum("ncfb,nf->ncb", nodes_here, chooser, precision=lax.Precision.HIGHEST)
    return leaf_table(selected, split_rows)


def on_device(binned, node_of, margin, labels, split_feature, split_bin):
    row_count, feat_count = binned.shape
    node_total = split_feature.shape[0]
    feat_start = lax.axis_index("feat") * feat_count
    probability = jax.nn.sigmoid(margin)
    gradient = (probability - labels).astype(jnp.bfloat16)
    hessian = (probability * (1.0 - probability)).astype(jnp.bfloat16)
    node_hot = node_of[:, None] == jnp.arange(node_total, dtype=jnp.int32)[None, :]
    hot_float = node_hot.astype(jnp.bfloat16)
    weights = jnp.stack([gradient[:, None] * hot_float, hessian[:, None] * hot_float], axis=2)
    weights = weights.reshape(row_count, 2 * node_total)
    row_feature = jnp.sum(jnp.where(node_hot, split_feature[None, :], 0), axis=1)
    row_cut = jnp.sum(jnp.where(node_hot, split_bin[None, :], 0), axis=1)
    local = row_feature - feat_start
    owned = (local >= 0) & (local < feat_count)
    column_hot = jnp.arange(feat_count, dtype=jnp.int32)[None, :] == local[:, None]
    row_value = jnp.sum(jnp.where(column_hot, binned, 0), axis=1)
    right_bits = ((row_value > row_cut) & owned).astype(jnp.int32)
    go_right = lax.psum(right_bits, "feat")
    bin_ids = jnp.arange(BINS, dtype=jnp.int32)
    group = 8

    def add_block(block_index, partial_value):
        columns = lax.dynamic_slice_in_dim(binned, block_index * group, group, 1)
        one_hot = (columns.T[:, :, None] == bin_ids[None, None, :]).astype(jnp.bfloat16)
        piece = jnp.einsum("rk,frb->kfb", weights, one_hot, preferred_element_type=jnp.float32)
        return lax.dynamic_update_slice_in_dim(partial_value, piece, block_index * group, 1)

    partial_value = lax.fori_loop(
        0,
        feat_count // group,
        add_block,
        jnp.zeros((2 * node_total, feat_count, BINS), jnp.float32),
    )
    partial_value = partial_value.reshape(node_total, 2, feat_count, BINS).astype(jnp.bfloat16)
    node_share = node_total // lax.axis_size("rows")
    node_start = lax.axis_index("rows") * node_share
    histogram = lax.psum_scatter(partial_value, "rows", scatter_dimension=0, tiled=True).astype(
        jnp.float32
    )
    mine_feature = lax.dynamic_slice_in_dim(split_feature, node_start, node_share, 0)
    mine_cut = lax.dynamic_slice_in_dim(split_bin, node_start, node_share, 0)
    table_part = node_sums(histogram, mine_feature, mine_cut, feat_start)
    placed = lax.dynamic_update_slice_in_dim(
        jnp.zeros((node_total, 4), jnp.float32), table_part, node_start, 0
    )
    table = lax.psum(placed, ("feat", "rows"))
    leaf_left = -table[:, 0] / (table[:, 1] + 1.0)
    leaf_right = -(table[:, 2] - table[:, 0]) / (table[:, 3] - table[:, 1] + 1.0)
    row_left = jnp.sum(jnp.where(node_hot, leaf_left[None, :], 0.0), axis=1)
    row_right = jnp.sum(jnp.where(node_hot, leaf_right[None, :], 0.0), axis=1)
    margin_out = margin + jnp.where(go_right == 1, row_right, row_left)
    child_out = 2 * node_of + go_right
    fresh = jax.nn.sigmoid(margin_out)
    grad_out = jnp.stack([fresh - labels, fresh * (1.0 - fresh)], axis=0)
    return (histogram, margin_out, child_out, grad_out)


def solution(mesh):
    in_specs = (P("rows", "feat"), P("rows"), P("rows"), P("rows"), P(), P())
    out_specs = (P("rows", None, "feat", None), P("rows"), P("rows"), P(None, "rows"))
    return jax.shard_map(
        on_device, mesh=mesh, in_specs=in_specs, out_specs=out_specs, check_vma=False
    )
```

profile of v0, /device:TPU:0, one launch (start us, length us, event | category | flops | bytes accessed | tf_op | source)
XLA Modules:
  0.0 146.1 jit_solution(7453625732831481488)
XLA Ops:
  7.2 0.8 subtract_convert_fusion
  8.0 1.1 compare_select_fusion.1
  9.1 0.6 pad_maximum_fusion
  9.7 0.1 reshape.186
  9.8 0.2 broadcast_in_dim.68
  10.1 35.7 %while.14 = (s32[]{:T(128)}, bf16[64,64,256]{2,0,1:T(8,128)(2,1)S(1)}, s32[2048,64]{0,1:T(8,128)S(1)}, bf16[2048,64]{0,1:T(8,128)(2,1)S(1)}, s32[]{:T(128)}, /*index=5*/s32[]{:T(128)}, s32[]{:T(128)}, s32[]{:T(128)}) while((s32[]{:T(128)}, bf16[64,64,256]{2,0,1:T(8,128)(2,1)S(1)}, s32[2048,64]{0,1:T(8,128)S(1)}, ...), condition=%wide.region_1.2_spmd.clone, body=%wide.region_0.1_spmd.clone.sunk | while | flops 541065216 | bytes 983187 | solution.py:55
  10.1 4.4 %fusion.21 = bf16[64,64,256]{2,0,1:T(8,128)(2,1)S(1)} fusion(bf16[64,64,256]{2,0,1:T(8,128)(2,1)S(1)} %get-tuple-element.167, s32[]{:T(128)S(6)} %select_n.51, s32[8,2048]{1,0:T(8,128)S(1)} %dynamic-slice_bitcast_fusion.2, bf16[2048,64]{0,1:T(8,128)(2,1)S(1)} %get-tuple-element.177), kind=kOutput, calls=%fused_computation.5.clone.1 | convolution fusion | flops 541065216 | bytes 851972 | tf_op jit(solution)/shard_map/while/body/eval_jaxpr/rk,frb->kfb/dot_general | solution.py:52
  14.6 4.4 %fusion.21 = bf16[64,64,256]{2,0,1:T(8,128)(2,1)S(1)} fusion(bf16[64,64,256]{2,0,1:T(8,128)(2,1)S(1)} %get-tuple-element.167, s32[]{:T(128)S(6)} %select_n.51, s32[8,2048]{1,0:T(8,128)S(1)} %dynamic-slice_bitcast_fusion.2, bf16[2048,64]{0,1:T(8,128)(2,1)S(1)} %get-tuple-element.177), kind=kOutput, calls=%fused_computation.5.clone.1 | convolution fusion | flops 541065216 | bytes 851972 | tf_op jit(solution)/shard_map/while/body/eval_jaxpr/rk,frb->kfb/dot_general | solution.py:52
  19.1 4.4 %fusion.21 = bf16[64,64,256]{2,0,1:T(8,128)(2,1)S(1)} fusion(bf16[64,64,256]{2,0,1:T(8,128)(2,1)S(1)} %get-tuple-element.167, s32[]{:T(128)S(6)} %select_n.51, s32[8,2048]{1,0:T(8,128)S(1)} %dynamic-slice_bitcast_fusion.2, bf16[2048,64]{0,1:T(8,128)(2,1)S(1)} %get-tuple-element.177), kind=kOutput, calls=%fused_computation.5.clone.1 | convolution fusion | flops 541065216 | bytes 851972 | tf_op jit(solution)/shard_map/while/body/eval_jaxpr/rk,frb->kfb/dot_general | solution.py:52
  23.5 4.4 %fusion.21 = bf16[64,64,256]{2,0,1:T(8,128)(2,1)S(1)} fusion(bf16[64,64,256]{2,0,1:T(8,128)(2,1)S(1)} %get-tuple-element.167, s32[]{:T(128)S(6)} %select_n.51, s32[8,2048]{1,0:T(8,128)S(1)} %dynamic-slice_bitcast_fusion.2, bf16[2048,64]{0,1:T(8,128)(2,1)S(1)} %get-tuple-element.177), kind=kOutput, calls=%fused_computation.5.clone.1 | convolution fusion | flops 541065216 | bytes 851972 | tf_op jit(solution)/shard_map/while/body/eval_jaxpr/rk,frb->kfb/dot_general | solution.py:52
  28.0 4.4 %fusion.21 = bf16[64,64,256]{2,0,1:T(8,128)(2,1)S(1)} fusion(bf16[64,64,256]{2,0,1:T(8,128)(2,1)S(1)} %get-tuple-element.167, s32[]{:T(128)S(6)} %select_n.51, s32[8,2048]{1,0:T(8,128)S(1)} %dynamic-slice_bitcast_fusion.2, bf16[2048,64]{0,1:T(8,128)(2,1)S(1)} %get-tuple-element.177), kind=kOutput, calls=%fused_computation.5.clone.1 | convolution fusion | flops 541065216 | bytes 851972 | tf_op jit(solution)/shard_map/while/body/eval_jaxpr/rk,frb->kfb/dot_general | solution.py:52
  32.5 4.4 %fusion.21 = bf16[64,64,256]{2,0,1:T(8,128)(2,1)S(1)} fusion(bf16[64,64,256]{2,0,1:T(8,128)(2,1)S(1)} %get-tuple-element.167, s32[]{:T(128)S(6)} %select_n.51, s32[8,2048]{1,0:T(8,128)S(1)} %dynamic-slice_bitcast_fusion.2, bf16[2048,64]{0,1:T(8,128)(2,1)S(1)} %get-tuple-element.177), kind=kOutput, calls=%fused_computation.5.clone.1 | convolution fusion | flops 541065216 | bytes 851972 | tf_op jit(solution)/shard_map/while/body/eval_jaxpr/rk,frb->kfb/dot_general | solution.py:52
  36.9 4.4 %fusion.21 = bf16[64,64,256]{2,0,1:T(8,128)(2,1)S(1)} fusion(bf16[64,64,256]{2,0,1:T(8,128)(2,1)S(1)} %get-tuple-element.167, s32[]{:T(128)S(6)} %select_n.51, s32[8,2048]{1,0:T(8,128)S(1)} %dynamic-slice_bitcast_fusion.2, bf16[2048,64]{0,1:T(8,128)(2,1)S(1)} %get-tuple-element.177), kind=kOutput, calls=%fused_computation.5.clone.1 | convolution fusion | flops 541065216 | bytes 851972 | tf_op jit(solution)/shard_map/while/body/eval_jaxpr/rk,frb->kfb/dot_general | solution.py:52
  41.4 4.4 %fusion.21 = bf16[64,64,256]{2,0,1:T(8,128)(2,1)S(1)} fusion(bf16[64,64,256]{2,0,1:T(8,128)(2,1)S(1)} %get-tuple-element.167, s32[]{:T(128)S(6)} %select_n.51, s32[8,2048]{1,0:T(8,128)S(1)} %dynamic-slice_bitcast_fusion.2, bf16[2048,64]{0,1:T(8,128)(2,1)S(1)} %get-tuple-element.177), kind=kOutput, calls=%fused_computation.5.clone.1 | convolution fusion | flops 541065216 | bytes 851972 | tf_op jit(solution)/shard_map/while/body/eval_jaxpr/rk,frb->kfb/dot_general | solution.py:52
  45.8 2.5 %copy.11 = bf16[64,64,256]{2,1,0:T(8,128)(2,1)} copy(bf16[64,64,256]{2,0,1:T(8,128)(2,1)S(1)} %get-tuple-element.98) | data formatting | bytes 4194304 | tf_op jit(solution)/shard_map/convert_element_type | solution.py:61
  48.4 0.6 copy-done.6
  49.0 0.1 dynamic_slice.14
  49.1 0.2 select_reduce_fusion.3
  49.3 0.1 select_reduce_fusion
  49.3 9.6 %psum.14 = s32[2048]{0:T(1024)S(1)} all-reduce(s32[2048]{0:T(1024)S(1)} %and_convert_fusion), channel_id=1, replica_groups=mesh['feat'=8,'rows'=4] {'feat'}, use_global_device_ids=true, to_apply=%region_6.7 | all-reduce | flops 2048 | bytes 16384 | tf_op jit(solution)/shard_map/psum | solution.py:45
  59.0 0.1 compare_and_fusion
  59.0 0.1 fusion.13
  59.1 0.1 fusion.11
  59.2 0.6 multiply_add_fusion
  59.8 35.3 %reduce-scatter.2.cloned.1.call-done = bf16[8,2,64,256]{3,2,1,0:T(8,128)(2,1)} async-done(((bf16[32,2,64,256]{3,2,1,0:T(8,128)(2,1)}), bf16[8,2,64,256]{3,2,1,0:T(8,128)(2,1)}) %reduce-scatter.2.cloned.1.call-update) | async-done | bytes 524304 | tf_op jit(solution)/shard_map/reduce_scatter | solution.py:64
  95.1 1.2 fusion.8
  96.3 0.1 fusion.7
  96.5 0.1 dynamic_update_slice.10
  96.6 39.7 %psum.15 = f32[32,4]{0,1:T(4,128)S(1)} all-reduce(f32[32,4]{0,1:T(4,128)S(1)} %dynamic_update_slice.10), channel_id=1, replica_groups=mesh['feat'=8,'rows'=4] {'feat','rows'}, use_global_device_ids=true, to_apply=%region_9.10 | all-reduce | flops 128 | bytes 1024 | tf_op jit(solution)/shard_map/psum | solution.py:73
  136.3 0.2 select_reduce_fusion.1
  136.5 0.6 pad_maximum_fusion.1
  137.1 2.1 %convert_element_type.34 = f32[8,2,64,256]{3,2,1,0:T(8,128)} convert(bf16[8,2,64,256]{3,2,1,0:T(8,128)(2,1)} %reduce-scatter.2.cloned.1.call-done) | non-fusion elementwise | flops 262144 | bytes 1572864 | tf_op jit(solution)/shard_map/convert_element_type | solution.py:64
  (30 shorter events, 0.2 us)
Async XLA Ops:
  7.2 2.9 %copy-start = (s32[2048,64]{0,1:T(8,128)S(1)}, s32[2048,64]{0,1:T(8,128)}, u32[]{:S(2)}) copy-start(s32[2048,64]{0,1:T(8,128)} %param.8) | copy-start | bytes 1572868
  7.2 87.9 %reduce-scatter.2.cloned.1.call-start = ((), (), s32[]{:S(2)}) async-start(), calls=%async_computation.1 | async-start | bytes 2621440 | tf_op jit(solution)/shard_map/reduce_scatter | solution.py:64
  48.3 0.7 copy-start.6
  48.4 0.7 copy-start.1
  48.4 0.7 copy-start.5
  48.4 88.1 %copy-start.2 = (f32[2048]{0:T(1024)S(1)}, f32[2048]{0:T(1024)}, u32[]{:S(2)}) copy-start(f32[2048]{0:T(1024)} %param.11) | copy-start | bytes 24580
  48.4 88.1 %copy-start.3 = (f32[2048]{0:T(1024)S(1)}, f32[2048]{0:T(1024)}, u32[]{:S(2)}) copy-start(f32[2048]{0:T(1024)} %param.10) | copy-start | bytes 24580
  136.5 2.8 %copy-start.4 = (f32[2048]{0:T(1024)}, f32[2048]{0:T(1024)S(1)}, u32[]{:S(2)}) copy-start(f32[2048]{0:T(1024)S(1)} %get-tuple-element.124) | copy-start | bytes 24580
Sparse Core Ops, SparseCore 0:
  48.5 46.5 reduce-scatter.1
where the time goes:
time: 147 us; the launch traced here: 146 us
  blocking collectives  49.3 us (34%)
  matrix products  36.6 us (25%)
  waiting for transfers between devices  35.4 us (24%)
  between operations  14.2 us (10%)
  other arithmetic  6.59 us (4%)
  local copies, waits for them, and re-layouts  3.82 us (3%)
    psum x1, blocking collectives, on_device(): table = lax.psum(placed, ('feat', 'rows'))  39.7 us
    dot_general x8, matrix products, add_block(): jnp.einsum('rk,frb->kfb', weights, one_hot, preferred_element_type=jnp.fl...  35.3 us
    reduce_scatter x1, waiting for transfers between devices, on_device(): lax.psum_scatter(partial_value, 'rows', scatter_dimension=0, tiled=True)  35.3 us
    psum x1, blocking collectives, on_device(): go_right = lax.psum(right_bits, 'feat')  9.61 us
  transfers between devices with their start and end apart: 1, of which 1 were waited for; matrix products, arithmetic and copies ran while one was open for 1% of the time, Pallas kernels for 0%

commit v1 on v0

v1 whole, which is shorter than its diff:
```python
import functools

import jax
import jax.numpy as jnp
from jax import lax
from jax.experimental import pallas as pl
from jax.experimental.pallas import tpu as pltpu
from jax.sharding import PartitionSpec as P

BINS = 256


def hist_kernel(sources, nodes, feats, raw_ref, out_ref, held, weights, total):
    row_count = raw_ref.shape[2]
    bin_ids = lax.broadcasted_iota(jnp.int32, (BINS, row_count), 0).astype(jnp.bfloat16)
    node_ids = lax.broadcasted_iota(jnp.int32, (2 * nodes, row_count), 0)
    for source in range(sources):
        block = raw_ref[source].astype(jnp.float32)
        held[...] = block
        grad = block[feats : feats + 1]
        hess = block[feats + 1 : feats + 2]
        node = block[feats + 2 : feats + 3].astype(jnp.int32)
        pair = jnp.where(node_ids < nodes, grad, hess)
        mine = jnp.where(node_ids < nodes, node_ids, node_ids - nodes) == node
        weights[...] = jnp.where(mine, pair, 0.0).astype(jnp.bfloat16)

        def add_feature(feat, carry):
            bins = held[pl.ds(feat, 1), :].astype(jnp.bfloat16)
            hot = jnp.where(bin_ids == bins, 1.0, 0.0).astype(jnp.bfloat16)
            piece = lax.dot_general(
                weights[...], hot, (((1,), (1,)), ((), ())), preferred_element_type=jnp.float32
            )
            if source == 0:
                total[feat] = piece
            else:
                total[feat] += piece
            return carry

        lax.fori_loop(0, feats, add_feature, 0)
    out_ref[...] = total[...].astype(out_ref.dtype)


def on_device(binned, node_of, margin, labels, split_feature, split_bin):
    row_count, feat_count = binned.shape
    node_total = split_feature.shape[0]
    sources = lax.axis_size("rows")
    feats = feat_count // sources
    share = node_total // sources
    feat_start = lax.axis_index("feat") * feat_count
    probability = jax.nn.sigmoid(margin)
    gradient = (probability - labels).astype(jnp.bfloat16)
    hessian = (probability * (1.0 - probability)).astype(jnp.bfloat16)
    node_hot = node_of[None, :] == jnp.arange(node_total, dtype=jnp.int32)[:, None]
    row_feature = jnp.sum(jnp.where(node_hot, split_feature[:, None], 0), axis=0)
    row_cut = jnp.sum(jnp.where(node_hot, split_bin[:, None], 0), axis=0)
    local = row_feature - feat_start
    binned_t = binned.T
    column_hot = jnp.arange(feat_count, dtype=jnp.int32)[:, None] == local[None, :]
    right_bits = jnp.sum(
        (column_hot & (binned_t > row_cut[None, :])).astype(jnp.int32), axis=0
    )
    go_right = lax.psum(right_bits, "feat")

    meta = jnp.stack([gradient, hessian, node_of.astype(jnp.bfloat16)], axis=0)
    raw = jnp.concatenate(
        [
            binned_t.astype(jnp.bfloat16).reshape(sources, feats, row_count),
            jnp.broadcast_to(meta[None], (sources, 3, row_count)),
        ],
        axis=1,
    )
    raw = lax.all_to_all(raw, "rows", 0, 0)
    whole = pl.pallas_call(
        functools.partial(hist_kernel, sources, node_total, feats),
        out_shape=jax.ShapeDtypeStruct((feats, 2 * node_total, BINS), jnp.bfloat16),
        in_specs=[pl.BlockSpec(memory_space=pltpu.VMEM)],
        out_specs=pl.BlockSpec(memory_space=pltpu.VMEM),
        scratch_shapes=[
            pltpu.VMEM((feats + 3, row_count), jnp.float32),
            pltpu.VMEM((2 * node_total, row_count), jnp.bfloat16),
            pltpu.VMEM((feats, 2 * node_total, BINS), jnp.float32),
        ],
        compiler_params=pltpu.CompilerParams(vmem_limit_bytes=32 * 1024 * 1024),
    )(raw)
    whole = whole.reshape(feats, 2, sources, share, BINS).transpose(2, 3, 1, 0, 4)
    whole = lax.all_to_all(whole, "rows", 0, 0)
    histogram = whole.transpose(1, 2, 0, 3, 4).reshape(share, 2, feat_count, BINS)
    histogram = histogram.astype(jnp.float32)

    values = jnp.stack([gradient, hessian], axis=0).astype(jnp.float32)
    both = jnp.concatenate([jnp.where(go_right[None, :] == 0, values, 0.0), values], axis=0)
    table = jnp.sum(jnp.where(node_hot[None], both[:, None, :], 0.0), axis=2)
    table = lax.psum(table, "rows")
    leaf_left = -table[0] / (table[1] + 1.0)
    leaf_right = -(table[2] - table[0]) / (table[3] - table[1] + 1.0)
    leaf = jnp.where(go_right[None, :] == 1, leaf_right[:, None], leaf_left[:, None])
    margin_out = margin + jnp.sum(jnp.where(node_hot, leaf, 0.0), axis=0)
    child_out = 2 * node_of + go_right
    fresh = jax.nn.sigmoid(margin_out)
    grad_out = jnp.stack([fresh - labels, fresh * (1.0 - fresh)], axis=0)
    return (histogram, margin_out, child_out, grad_out)


def solution(mesh):
    in_specs = (P("rows", "feat"), P("rows"), P("rows"), P("rows"), P(), P())
    out_specs = (P("rows", None, "feat", None), P("rows"), P("rows"), P(None, "rows"))
    return jax.shard_map(
        on_device, mesh=mesh, in_specs=in_specs, out_specs=out_specs, check_vma=False
    )
```

time: 147 us -> 82.4 us (0.56)
  matrix products: 36.6 us -> 0 us
  Pallas kernels: 0 us -> 32 us
  blocking collectives: 49.3 us -> 21.9 us
  waiting for transfers between devices: 35.4 us -> 9.89 us
  between operations: 14.2 us -> 0.84 us
  starting transfers between devices: 0.04 us -> 8.34 us
  other arithmetic: 6.59 us -> 4.76 us
    dot_general x9 -> x0, matrix products: 36.6 us -> none  [the longest x8 35.3 us: add_block(): jnp.einsum('rk,frb->kfb', weights, one_hot, preferred_element_type=jnp.fl...]
    reduce_scatter x1 -> x0, waiting for transfers between devices: 35.3 us -> none  [on_device(): lax.psum_scatter(partial_value, 'rows', scatter_dimension=0, tiled=True)]
    pallas_call x0 -> x1, Pallas kernels: none -> 32 us  [on_device(): pl.pallas_call(functools.partial(hist_kernel, sources, node_total, feats)...]
    psum x1, blocking collectives: 39.7 us -> 12.3 us  [on_device(): table = lax.psum(table, 'rows')]
    all_to_all x0 -> x2, waiting for transfers between devices: none -> 9.89 us  [the longest x1 9.89 us: on_device(): whole = lax.all_to_all(whole, 'rows', 0, 0)]
    all_to_all x0 -> x2, starting transfers between devices: none -> 8.34 us  [the longest x1 4.87 us: on_device(): raw = lax.all_to_all(raw, 'rows', 0, 0)]
    unnamed x14 -> x15, local copies, waits for them, and re-layouts: 0.63 us -> 3.39 us
    convert_element_type x1 -> x0, local copies, waits for them, and re-layouts: 2.53 us -> none  [on_device(): partial_value.reshape(node_total, 2, feat_count, BINS).astype(jnp.bfloat16)]
  transfers between devices with their start and end apart: 1 -> 2, of which waited for: 1 -> 1; matrix products, arithmetic and copies ran while one was open for 1% -> 1% of each run, Pallas kernels for 0% -> 0%
where the time goes in v1:
time: 82.4 us; the launch traced here: 82 us
  Pallas kernels  32 us (39%)
  blocking collectives  21.9 us (27%)
  waiting for transfers between devices  9.89 us (12%)
  starting transfers between devices  8.34 us (10%)
  other arithmetic  4.76 us (6%)
  local copies, waits for them, and re-layouts  4.27 us (5%)
  between operations  0.84 us (1%)
    pallas_call x1, Pallas kernels, on_device(): pl.pallas_call(functools.partial(hist_kernel, sources, node_total, feats)...  32 us
    psum x1, blocking collectives, on_device(): table = lax.psum(table, 'rows')  12.3 us
    all_to_all x1, waiting for transfers between devices, on_device(): whole = lax.all_to_all(whole, 'rows', 0, 0)  9.89 us
    psum x1, blocking collectives, on_device(): go_right = lax.psum(right_bits, 'feat')  9.61 us
    all_to_all x1, starting transfers between devices, on_device(): raw = lax.all_to_all(raw, 'rows', 0, 0)  4.87 us
    all_to_all x1, starting transfers between devices, on_device(): whole = lax.all_to_all(whole, 'rows', 0, 0)  3.47 us
    unnamed x15, local copies, waits for them, and re-layouts  3.39 us
  transfers between devices with their start and end apart: 2, of which 1 were waited for; matrix products, arithmetic and copies ran while one was open for 1% of the time, Pallas kernels for 0%

profile of v1, /device:TPU:0, one launch (start us, length us, event | category | flops | bytes accessed | tf_op | source)
XLA Modules:
  0.0 82.0 jit_solution(14047581989065419530)
XLA Ops:
  0.6 0.0 copy-start
  0.6 0.8 subtract_convert_fusion
  1.5 0.0 copy-start.1
  1.5 1.1 %convert_element_type.30 = bf16[2048,64]{0,1:T(8,128)(2,1)S(1)} convert(s32[2048,64]{0,1:T(8,128)} %param.6) | non-fusion elementwise | flops 131072 | bytes 786432 | tf_op jit(solution)/shard_map/convert_element_type | solution.py:67
  2.6 0.0 copy-start.5
  2.6 0.0 copy-start.6
  2.6 0.0 copy-done.1
  2.6 0.6 copy-done.5
  3.2 0.0 copy-done.6
  3.2 0.2 select_reduce_fusion.3
  3.4 0.1 convert_reduce_fusion
  3.5 9.6 %psum.14 = s32[2048]{0:T(1024)S(1)} all-reduce(s32[2048]{0:T(1024)S(1)} %convert_reduce_fusion), channel_id=1, replica_groups=mesh['feat'=8,'rows'=4] {'feat'}, use_global_device_ids=true, to_apply=%region_3.4 | all-reduce | flops 2048 | bytes 16384 | tf_op jit(solution)/shard_map/psum | solution.py:62
  13.1 0.6 multiply_add_fusion
  13.8 0.8 pad_maximum_fusion
  14.6 4.9 %all-to-all-start = ((bf16[4,19,2048]{2,1,0:T(8,128)(2,1)}), bf16[4,19,2048]{2,1,0:T(8,128)(2,1)S(1)}, u32[]{:S(2)}, u32[]{:S(2)}) async-start(bf16[4,19,2048]{2,1,0:T(8,128)(2,1)} %pad_maximum_fusion), calls=%async_computation | async-start | bytes 786432 | tf_op jit(solution)/shard_map/all_to_all | solution.py:72
  19.6 0.2 select_reduce_fusion
  19.8 12.3 %psum.15 = f32[4,32]{1,0:T(4,128)S(1)} all-reduce(f32[4,32]{1,0:T(4,128)S(1)} %select_reduce_fusion), channel_id=1, replica_groups=mesh['feat'=8,'rows'=4] {'rows'}, use_global_device_ids=true, to_apply=%region_5.6 | all-reduce | flops 128 | bytes 1024 | tf_op jit(solution)/shard_map/psum | solution.py:93
  32.1 0.0 all-to-all-done.raw_ref
  32.1 32.0 %shard_map.93 = bf16[16,64,256]{2,1,0:T(8,128)(2,1)S(1)} custom-call(bf16[4,19,2048]{2,1,0:T(8,128)(2,1)S(1)} %all-to-all-done.raw_ref), custom_call_target="tpu_custom_call" | custom-call | tf_op jit(solution)/shard_map/pallas_call | solution.py:73
  64.1 0.8 %copy.16 = bf16[16,2,4,8,256]{4,3,1,0,2:T(8,128)(2,1)} copy(bf16[16,2,4,8,256]{4,3,2,1,0:T(8,128)(2,1)S(1)} %bitcast.18) | data formatting | bytes 1048576 | tf_op jit(solution)/shard_map/reshape | solution.py:85
  64.9 3.5 %all-to-all-start.1 = ((bf16[4,8,2,16,256]{4,1,2,3,0:T(8,128)(2,1)}), bf16[4,8,2,16,256]{4,1,2,3,0:T(8,128)(2,1)S(1)}, u32[]{:S(2)}, u32[]{:S(2)}) async-start(bf16[4,8,2,16,256]{4,1,2,3,0:T(8,128)(2,1)} %bitcast.17), calls=%async_computation.1 | async-start | bytes 1048576 | tf_op jit(solution)/shard_map/all_to_all | solution.py:86
  68.4 0.0 copy-start.2
  68.4 0.0 copy-start.3
  68.4 0.1 select_reduce_fusion.1
  68.6 0.5 copy-done.2
  69.1 0.0 copy-done.3
  69.1 0.0 copy-start.4
  69.2 0.6 copy-done.4
  69.8 0.6 pad_maximum_fusion.3
  70.4 9.9 %all-to-all-done.1 = bf16[4,8,2,16,256]{4,1,2,3,0:T(8,128)(2,1)S(1)} async-done(((bf16[4,8,2,16,256]{4,1,2,3,0:T(8,128)(2,1)}), bf16[4,8,2,16,256]{4,1,2,3,0:T(8,128)(2,1)S(1)}, u32[]{:S(2)}, u32[]{:S(2)}) %all-to-all-start.1) | async-done | bytes 524320 | tf_op jit(solution)/shard_map/all_to_all | solution.py:86
  80.3 0.1 convert_element_type.41
  80.4 1.6 %copy.14 = f32[8,2,64,256]{3,2,1,0:T(8,128)} copy(f32[8,2,64,256]{3,0,1,2:T(8,128)S(1)} %bitcast.19) | data formatting | bytes 2097152
  (15 shorter events, 0.2 us)
Async XLA Ops:
  0.6 2.8 %copy-start = (s32[2048,64]{0,1:T(8,128)S(1)}, s32[2048,64]{0,1:T(8,128)}, u32[]{:S(2)}) copy-start(s32[2048,64]{0,1:T(8,128)} %param.6) | copy-start | bytes 1572868
  1.5 1.1 %copy-start.1 = (s32[2048]{0:T(1024)S(1)}, s32[2048]{0:T(1024)}, u32[]{:S(2)}) copy-start(s32[2048]{0:T(1024)} %param.7) | copy-start | bytes 24580
  2.6 0.7 copy-start.5
  2.6 0.7 copy-start.6
  14.6 17.5 %all-to-all-start = ((bf16[4,19,2048]{2,1,0:T(8,128)(2,1)}), bf16[4,19,2048]{2,1,0:T(8,128)(2,1)S(1)}, u32[]{:S(2)}, u32[]{:S(2)}) async-start(bf16[4,19,2048]{2,1,0:T(8,128)(2,1)} %pad_maximum_fusion), calls=%async_computation | async-start | bytes 786432 | tf_op jit(solution)/shard_map/all_to_all | solution.py:72
  64.9 15.3 %all-to-all-start.1 = ((bf16[4,8,2,16,256]{4,1,2,3,0:T(8,128)(2,1)}), bf16[4,8,2,16,256]{4,1,2,3,0:T(8,128)(2,1)S(1)}, u32[]{:S(2)}, u32[]{:S(2)}) async-start(bf16[4,8,2,16,256]{4,1,2,3,0:T(8,128)(2,1)} %bitcast.17), calls=%async_computation.1 | async-start | bytes 1048576 | tf_op jit(solution)/shard_map/all_to_all | solution.py:86
  68.4 0.7 copy-start.2
  68.4 0.7 copy-start.3
  69.1 0.6 copy-start.4

commit v2 on v1

v2 whole, which is shorter than its diff:
```python
import functools

import jax
import jax.numpy as jnp
from jax import lax
from jax.experimental import pallas as pl
from jax.experimental.pallas import tpu as pltpu
from jax.sharding import PartitionSpec as P

BINS = 256
GROUP = 4
PAIR = 2
MESH = pl.DeviceIdType.MESH


def level_kernel(
    sources, columns, nodes, feats, bins_ref, meta_ref, bits_ref,
    hist_ref, go_ref, table_ref,
    raw_in, meta_in, bits_in, table_in, held, weights, total, staged,
    raw_send, raw_recv, meta_send, meta_recv, bits_send, bits_recv,
    table_send, table_recv, hist_send, hist_recv,
):
    row_count = bins_ref.shape[2]
    me = lax.axis_index("rows")
    column = lax.axis_index("feat")
    share = 2 * nodes // sources
    groups = feats // GROUP

    def row_peer(step):
        return lax.rem(me + step, sources)

    def feat_peer(step):
        return lax.rem(column + step, columns)

    barrier = pltpu.get_barrier_semaphore()
    for step in range(1, sources):
        pl.semaphore_signal(
            barrier, inc=1, device_id={"rows": row_peer(step)}, device_id_type=MESH
        )

    def greet(step, carry):
        pl.semaphore_signal(
            barrier, inc=1, device_id={"feat": feat_peer(step)}, device_id_type=MESH
        )
        return carry

    lax.fori_loop(1, columns, greet, 0)
    pl.semaphore_wait(barrier, sources - 1 + columns - 1)

    def raw_copy(step, slot, peer):
        return pltpu.make_async_remote_copy(
            src_ref=bins_ref.at[peer], dst_ref=raw_in.at[slot],
            send_sem=raw_send.at[step], recv_sem=raw_recv.at[slot],
            device_id={"rows": peer}, device_id_type=MESH,
        )

    def meta_copy(step, slot, peer):
        return pltpu.make_async_remote_copy(
            src_ref=meta_ref, dst_ref=meta_in.at[slot],
            send_sem=meta_send.at[step], recv_sem=meta_recv.at[slot],
            device_id={"rows": peer}, device_id_type=MESH,
        )

    def bits_copy(step, slot, peer):
        return pltpu.make_async_remote_copy(
            src_ref=bits_ref, dst_ref=bits_in.at[slot],
            send_sem=bits_send.at[step], recv_sem=bits_recv.at[slot],
            device_id={"feat": peer}, device_id_type=MESH,
        )

    def table_copy(step, slot, peer):
        return pltpu.make_async_remote_copy(
            src_ref=table_ref, dst_ref=table_in.at[slot],
            send_sem=table_send.at[step], recv_sem=table_recv.at[slot],
            device_id={"rows": peer}, device_id_type=MESH,
        )

    def hist_copy(step, slot, peer, group):
        part = pl.ds(group * GROUP, GROUP)
        return pltpu.make_async_remote_copy(
            src_ref=staged.at[peer, part], dst_ref=hist_ref.at[slot, part],
            send_sem=hist_send.at[step, group], recv_sem=hist_recv.at[slot, group],
            device_id={"rows": peer}, device_id_type=MESH,
        )

    def send_bits(step, carry):
        bits_copy(step, column, feat_peer(step)).start()
        return carry

    lax.fori_loop(1, columns, send_bits, 0)
    for step in range(1, sources):
        meta_copy(step, me, row_peer(step)).start()
        raw_copy(step, me, row_peer(step)).start()

    bin_ids = lax.broadcasted_iota(jnp.int32, (BINS, row_count), 0)
    cells = lax.broadcasted_iota(jnp.int32, (2 * nodes, row_count), 0)
    cell_node = cells // 2
    is_grad = cells % 2 == 0

    def set_block(bins, meta):
        held[...] = bins.astype(jnp.float32).astype(jnp.int32)
        node = meta[2:3].astype(jnp.int32)
        pair = jnp.where(is_grad, meta[0:1], meta[1:2])
        weights[...] = jnp.where(cell_node == node, pair, 0.0).astype(jnp.bfloat16)

    def piece_of(feat):
        hot = (bin_ids == held[pl.ds(feat, 1), :]).astype(jnp.float32).astype(jnp.bfloat16)
        return lax.dot_general(
            weights[...], hot, (((1,), (1,)), ((), ())), preferred_element_type=jnp.float32
        )

    def add_block(first):
        def add_pair(index, carry):
            for offset in range(PAIR):
                feat = index * PAIR + offset
                if first:
                    total[feat] = piece_of(feat)
                else:
                    total[feat] += piece_of(feat)
            return carry

        lax.fori_loop(0, feats // PAIR, add_pair, 0)

    set_block(bins_ref[me], meta_ref[...])
    add_block(True)

    go_ref[...] = bits_ref[...]

    def take_bits(step, carry):
        peer = feat_peer(step)
        bits_copy(step, peer, peer).wait_recv()
        go_ref[...] += bits_in[peer]
        return carry

    lax.fori_loop(1, columns, take_bits, 0)
    node = meta_ref[2:3].astype(jnp.int32)
    mine = lax.broadcasted_iota(jnp.int32, (nodes, row_count), 0) == node
    left = go_ref[...] == 0
    lanes = lax.broadcasted_iota(jnp.int32, (nodes, 128), 1)
    table = jnp.zeros((nodes, 128), jnp.float32)
    for index in range(4):
        value = meta_ref[index % 2 : index % 2 + 1]
        if index < 2:
            value = jnp.where(left, value, 0.0)
        summed = jnp.sum(jnp.where(mine, value, 0.0), axis=1, keepdims=True)
        table = jnp.where(lanes == index, summed, table)
    table_ref[...] = table
    for step in range(1, sources):
        table_copy(step, me, row_peer(step)).start()

    for step in range(1, sources):
        peer = row_peer(step)
        meta_copy(step, peer, peer).wait_recv()
        raw_copy(step, peer, peer).wait_recv()
        set_block(raw_in[peer], meta_in[peer])
        if step < sources - 1:
            add_block(False)

    def finish(group, carry):
        for offset in range(GROUP):
            feat = group * GROUP + offset
            done = (total[feat] + piece_of(feat)).astype(jnp.bfloat16)
            for dest in range(sources):
                staged[dest, feat] = done[dest * share : (dest + 1) * share]
        for step in range(1, sources):
            hist_copy(step, me, row_peer(step), group).start()
        return carry

    lax.fori_loop(0, groups, finish, 0)
    hist_ref[me] = staged[me]

    def end_bits(step, carry):
        bits_copy(step, column, feat_peer(step)).wait_send()
        return carry

    lax.fori_loop(1, columns, end_bits, 0)
    for step in range(1, sources):
        peer = row_peer(step)
        meta_copy(step, me, peer).wait_send()
        raw_copy(step, me, peer).wait_send()
        table_copy(step, me, peer).wait_send()
    for step in range(1, sources):
        peer = row_peer(step)
        table_copy(step, peer, peer).wait_recv()
        table_ref[...] += table_in[peer]
    for step in range(1, sources):
        peer = row_peer(step)

        def end_group(group, carry):
            hist_copy(step, me, peer, group).wait_send()
            hist_copy(step, peer, peer, group).wait_recv()
            return carry

        lax.fori_loop(0, groups, end_group, 0)


def on_device(binned, node_of, margin, labels, split_feature, split_bin):
    row_count, feat_count = binned.shape
    nodes = split_feature.shape[0]
    sources = lax.axis_size("rows")
    columns = lax.axis_size("feat")
    feats = feat_count // sources
    share = 2 * nodes // sources
    feat_start = lax.axis_index("feat") * feat_count
    probability = jax.nn.sigmoid(margin)
    gradient = (probability - labels).astype(jnp.bfloat16)
    hessian = (probability * (1.0 - probability)).astype(jnp.bfloat16)
    node_hot = node_of[None, :] == jnp.arange(nodes, dtype=jnp.int32)[:, None]
    row_feature = jnp.sum(jnp.where(node_hot, split_feature[:, None], 0), axis=0)
    row_cut = jnp.sum(jnp.where(node_hot, split_bin[:, None], 0), axis=0)
    local = row_feature - feat_start
    binned_t = binned.T
    column_hot = jnp.arange(feat_count, dtype=jnp.int32)[:, None] == local[None, :]
    right_bits = jnp.sum(
        (column_hot & (binned_t > row_cut[None, :])).astype(jnp.int32), axis=0, keepdims=True
    )
    bins = binned_t.astype(jnp.bfloat16).reshape(sources, feats, row_count)
    meta = jnp.stack(
        [gradient.astype(jnp.float32), hessian.astype(jnp.float32), node_of.astype(jnp.float32)]
    )
    vmem = pl.BlockSpec(memory_space=pltpu.VMEM)
    dma = pltpu.SemaphoreType.DMA
    hist, go_right, table = pl.pallas_call(
        functools.partial(level_kernel, sources, columns, nodes, feats),
        out_shape=[
            jax.ShapeDtypeStruct((sources, feats, share, BINS), jnp.bfloat16),
            jax.ShapeDtypeStruct((1, row_count), jnp.int32),
            jax.ShapeDtypeStruct((nodes, 128), jnp.float32),
        ],
        in_specs=[vmem] * 3,
        out_specs=[vmem] * 3,
        scratch_shapes=[
            pltpu.VMEM((sources, feats, row_count), jnp.bfloat16),
            pltpu.VMEM((sources, 3, row_count), jnp.float32),
            pltpu.VMEM((columns, 1, row_count), jnp.int32),
            pltpu.VMEM((sources, nodes, 128), jnp.float32),
            pltpu.VMEM((feats, row_count), jnp.int32),
            pltpu.VMEM((2 * nodes, row_count), jnp.bfloat16),
            pltpu.VMEM((feats, 2 * nodes, BINS), jnp.float32),
            pltpu.VMEM((sources, feats, share, BINS), jnp.bfloat16),
            dma((sources,)),
            dma((sources,)),
            dma((sources,)),
            dma((sources,)),
            dma((columns,)),
            dma((columns,)),
            dma((sources,)),
            dma((sources,)),
            dma((sources, feats // GROUP)),
            dma((sources, feats // GROUP)),
        ],
        compiler_params=pltpu.CompilerParams(
            collective_id=0, has_side_effects=True, vmem_limit_bytes=40 * 1024 * 1024
        ),
    )(bins, meta, right_bits)
    histogram = hist.transpose(2, 0, 1, 3).reshape(nodes // sources, 2, feat_count, BINS)
    histogram = histogram.astype(jnp.float32)

    go_right = go_right[0]
    leaf_left = -table[:, 0] / (table[:, 1] + 1.0)
    leaf_right = -(table[:, 2] - table[:, 0]) / (table[:, 3] - table[:, 1] + 1.0)
    leaf = jnp.where(go_right[None, :] == 1, leaf_right[:, None], leaf_left[:, None])
    margin_out = margin + jnp.sum(jnp.where(node_hot, leaf, 0.0), axis=0)
    child_out = 2 * node_of + go_right
    fresh = jax.nn.sigmoid(margin_out)
    grad_out = jnp.stack([fresh - labels, fresh * (1.0 - fresh)], axis=0)
    return (histogram, margin_out, child_out, grad_out)


def solution(mesh):
    in_specs = (P("rows", "feat"), P("rows"), P("rows"), P("rows"), P(), P())
    out_specs = (P("rows", None, "feat", None), P("rows"), P("rows"), P(None, "rows"))
    return jax.shard_map(
        on_device, mesh=mesh, in_specs=in_specs, out_specs=out_specs, check_vma=False
    )
```

time: 82.4 us -> 47.9 us (0.58)
  blocking collectives: 21.9 us -> 0 us
  waiting for transfers between devices: 9.89 us -> 0 us
  Pallas kernels: 32 us -> 40.7 us
  starting transfers between devices: 8.34 us -> 0 us
  other arithmetic: 4.76 us -> 3.17 us
  local copies, waits for them, and re-layouts: 4.27 us -> 2.92 us
    psum x2 -> x0, blocking collectives: 21.9 us -> none  [the longest x1 12.3 us: on_device(): table = lax.psum(table, 'rows')]
    all_to_all x2 -> x0, waiting for transfers between devices: 9.89 us -> none  [the longest x1 9.89 us: on_device(): whole = lax.all_to_all(whole, 'rows', 0, 0)]
    pallas_call x1, Pallas kernels: 32 us -> 40.7 us  [on_device(): pl.pallas_call(functools.partial(level_kernel, sources, columns, nodes, f...]
    all_to_all x2 -> x0, starting transfers between devices: 8.34 us -> none  [the longest x1 4.87 us: on_device(): raw = lax.all_to_all(raw, 'rows', 0, 0)]
    reshape x1 -> x0, local copies, waits for them, and re-layouts: 0.84 us -> none  [on_device(): whole.reshape(feats, 2, sources, share, BINS).transpose(2, 3, 1, 0, 4)]
    convert_element_type x3 -> x2, other arithmetic: 1.88 us -> 1.14 us  [the longest x1 1.13 us: on_device(): bins = binned_t.astype(jnp.bfloat16).reshape(sources, feats, row_count)]
  transfers between devices with their start and end apart: 2 -> 0, of which waited for: 1 -> 0; matrix products, arithmetic and copies ran while one was open for 1% -> 0% of each run, Pallas kernels for 0% -> 0%
where the time goes in v2:
time: 47.9 us; the launch traced here: 47.6 us
  Pallas kernels  40.7 us (85%)
  other arithmetic  3.17 us (7%)
  local copies, waits for them, and re-layouts  2.92 us (6%)
  between operations  0.78 us (2%)
    pallas_call x1, Pallas kernels, on_device(): pl.pallas_call(functools.partial(level_kernel, sources, columns, nodes, f...  40.7 us
    unnamed x15, local copies, waits for them, and re-layouts  2.92 us
    convert_element_type x1, other arithmetic, on_device(): bins = binned_t.astype(jnp.bfloat16).reshape(sources, feats, row_count)  1.13 us

profile of v2, /device:TPU:0, one launch (start us, length us, event | category | flops | bytes accessed | tf_op | source)
XLA Modules:
  0.0 47.6 jit_solution(16717142984635799575)
XLA Ops:
  0.6 0.0 copy-start
  0.6 0.0 copy-start.1
  0.7 1.1 %convert_element_type.29 = bf16[2048,64]{0,1:T(8,128)(2,1)S(1)} convert(s32[2048,64]{0,1:T(8,128)} %param.6) | non-fusion elementwise | flops 131072 | bytes 786432 | tf_op jit(solution)/shard_map/convert_element_type | solution.py:217
  1.8 0.0 copy-done.1
  1.8 0.0 copy-start.3
  1.8 0.0 copy-start.4
  1.8 0.7 %copy-done.3 = f32[2048]{0:T(1024)S(1)} copy-done((f32[2048]{0:T(1024)S(1)}, f32[2048]{0:T(1024)}, u32[]{:S(2)}) %copy-start.3) | copy-done | bytes 8216
  2.5 0.0 copy-done.4
  2.5 0.0 copy-start.5
  2.5 0.0 copy-start.6
  2.6 0.6 %copy-done.5 = s32[32]{0:T(128)S(1)} copy-done((s32[32]{0:T(128)S(1)}, s32[32]{0:T(128)}, u32[]{:S(2)}) %copy-start.5) | copy-done | bytes 152
  3.2 0.0 copy-done.6
  3.2 0.2 select_reduce_fusion.2
  3.4 0.0 copy-done
  3.4 0.1 convert_reduce_fusion
  3.5 40.7 %shard_map.93 = (bf16[4,16,16,256]{3,2,1,0:T(8,128)(2,1)S(1)}, s32[1,2048]{1,0:T(1,128)S(1)}, f32[32,128]{1,0:T(8,128)S(1)}) custom-call(bf16[4,16,2048]{2,1,0:T(8,128)(2,1)S(1)} %bitcast.15, f32[3,2048]{1,0:T(4,128)S(1)} %pad_maximum_fusion.meta_ref, s32[1,2048]{1,0:T(1,128)S(1)} %bitcast.16), custom_call_target="tpu_custom_call" | custom-call | tf_op jit(solution)/shard_map/pallas_call | solution.py:223
  44.2 0.1 convert_bitcast_fusion
  44.4 1.6 %copy.13 = f32[16,4,16,256]{3,2,1,0:T(8,128)} copy(f32[16,4,16,256]{3,0,2,1:T(8,128)S(1)} %convert_bitcast_fusion) | data formatting | bytes 2097152
  46.0 0.2 fusion.2
  46.2 0.1 select_reduce_fusion
  46.3 0.0 copy-start.2
  46.4 0.6 %multiply_add_fusion = s32[2048]{0:T(1024)} fusion(s32[2048]{0:T(1024)S(1)} %bitcast.17, s32[2048]{0:T(1024)S(1)} %copy-done.1), kind=kLoop, calls=%fused_computation.19 | loop fusion | flops 4096 | bytes 24576 | tf_op jit(solution)/shard_map/add | solution.py:264
  47.0 0.0 copy-done.2
  47.0 0.6 %pad_maximum_fusion.1 = f32[2,2048]{1,0:T(2,128)} fusion(f32[1,2048]{1,0:T(1,128)S(1)} %bitcast.23, f32[1,2048]{1,0:T(1,128)S(1)} %bitcast.20), kind=kLoop, calls=%fused_computation.10 | loop fusion | flops 4096 | bytes 32768 | tf_op jit(solution)/shard_map/stack | solution.py:266
  (7 shorter events, 0.1 us)
Async XLA Ops:
  0.6 2.7 %copy-start = (s32[2048,64]{0,1:T(8,128)S(1)}, s32[2048,64]{0,1:T(8,128)}, u32[]{:S(2)}) copy-start(s32[2048,64]{0,1:T(8,128)} %param.6) | copy-start | bytes 1572868
  0.6 1.1 %copy-start.1 = (s32[2048]{0:T(1024)S(1)}, s32[2048]{0:T(1024)}, u32[]{:S(2)}) copy-start(s32[2048]{0:T(1024)} %param.7) | copy-start | bytes 24580
  1.8 0.7 %copy-start.3 = (f32[2048]{0:T(1024)S(1)}, f32[2048]{0:T(1024)}, u32[]{:S(2)}) copy-start(f32[2048]{0:T(1024)} %param.9) | copy-start | bytes 24580
  1.8 0.7 %copy-start.4 = (f32[2048]{0:T(1024)S(1)}, f32[2048]{0:T(1024)}, u32[]{:S(2)}) copy-start(f32[2048]{0:T(1024)} %param.8) | copy-start | bytes 24580
  2.5 0.7 %copy-start.5 = (s32[32]{0:T(128)S(1)}, s32[32]{0:T(128)}, u32[]{:S(2)}) copy-start(s32[32]{0:T(128)} %param.10) | copy-start | bytes 388
  2.5 0.7 %copy-start.6 = (s32[32]{0:T(128)S(1)}, s32[32]{0:T(128)}, u32[]{:S(2)}) copy-start(s32[32]{0:T(128)} %param.11) | copy-start | bytes 388
  46.3 0.6 %copy-start.2 = (f32[2048]{0:T(1024)}, f32[2048]{0:T(1024)S(1)}, u32[]{:S(2)}) copy-start(f32[2048]{0:T(1024)S(1)} %get-tuple-element.27) | copy-start | bytes 24580

commit v3 on v2

--- a/solution.py
+++ b/solution.py
@@ -9,7 +9,9 @@
 
 BINS = 256
 GROUP = 4
-PAIR = 2
+PAIR = 4
+SCALE = 256.0
+FINE = 16.0
 MESH = pl.DeviceIdType.MESH
 
 
@@ -92,19 +94,25 @@
         meta_copy(step, me, row_peer(step)).start()
         raw_copy(step, me, row_peer(step)).start()
 
-    bin_ids = lax.broadcasted_iota(jnp.int32, (BINS, row_count), 0)
+    bin_ids = lax.broadcasted_iota(jnp.int32, (BINS, row_count), 0).astype(jnp.bfloat16)
     cells = lax.broadcasted_iota(jnp.int32, (2 * nodes, row_count), 0)
     cell_node = cells // 2
     is_grad = cells % 2 == 0
 
     def set_block(bins, meta):
-        held[...] = bins.astype(jnp.float32).astype(jnp.int32)
+        held[...] = bins.astype(jnp.float32)
         node = meta[2:3].astype(jnp.int32)
         pair = jnp.where(is_grad, meta[0:1], meta[1:2])
-        weights[...] = jnp.where(cell_node == node, pair, 0.0).astype(jnp.bfloat16)
+        value = jnp.where(cell_node == node, pair * SCALE, 0.0)
+        coarse = value.astype(jnp.float8_e4m3fn)
+        rest = (value - coarse.astype(jnp.float32)) * FINE
+        weights[: 2 * nodes] = coarse
+        weights[2 * nodes :] = rest.astype(jnp.float8_e4m3fn)
 
     def piece_of(feat):
-        hot = (bin_ids == held[pl.ds(feat, 1), :]).astype(jnp.float32).astype(jnp.bfloat16)
+        bins = held[pl.ds(feat, 1), :].astype(jnp.bfloat16)
+        hot = jnp.where(bin_ids == bins, jnp.bfloat16(1), jnp.bfloat16(0))
+        hot = hot.astype(jnp.float8_e4m3fn)
         return lax.dot_general(
             weights[...], hot, (((1,), (1,)), ((), ())), preferred_element_type=jnp.float32
         )
@@ -159,7 +167,9 @@
     def finish(group, carry):
         for offset in range(GROUP):
             feat = group * GROUP + offset
-            done = (total[feat] + piece_of(feat)).astype(jnp.bfloat16)
+            both = total[feat] + piece_of(feat)
+            done = both[: 2 * nodes] + both[2 * nodes :] * (1.0 / FINE)
+            done = (done * (1.0 / SCALE)).astype(jnp.bfloat16)
             for dest in range(sources):
                 staged[dest, feat] = done[dest * share : (dest + 1) * share]
         for step in range(1, sources):
@@ -234,9 +244,9 @@
             pltpu.VMEM((sources, 3, row_count), jnp.float32),
             pltpu.VMEM((columns, 1, row_count), jnp.int32),
             pltpu.VMEM((sources, nodes, 128), jnp.float32),
-            pltpu.VMEM((feats, row_count), jnp.int32),
-            pltpu.VMEM((2 * nodes, row_count), jnp.bfloat16),
-            pltpu.VMEM((feats, 2 * nodes, BINS), jnp.float32),
+            pltpu.VMEM((feats, row_count), jnp.float32),
+            pltpu.VMEM((4 * nodes, row_count), jnp.float8_e4m3fn),
+            pltpu.VMEM((feats, 4 * nodes, BINS), jnp.float32),
             pltpu.VMEM((sources, feats, share, BINS), jnp.bfloat16),
             dma((sources,)),
             dma((sources,)),

time: 47.9 us -> 40.9 us (0.85)
  Pallas kernels: 40.7 us -> 33.7 us
    pallas_call x1, Pallas kernels: 40.7 us -> 33.7 us  [on_device(): pl.pallas_call(functools.partial(level_kernel, sources, columns, nodes, f...]
where the time goes in v3:
time: 40.9 us; the launch traced here: 40.6 us
  Pallas kernels  33.7 us (82%)
  other arithmetic  3.17 us (8%)
  local copies, waits for them, and re-layouts  2.92 us (7%)
  between operations  0.78 us (2%)
    pallas_call x1, Pallas kernels, on_device(): pl.pallas_call(functools.partial(level_kernel, sources, columns, nodes, f...  33.7 us
    unnamed x15, local copies, waits for them, and re-layouts  2.92 us
    convert_element_type x1, other arithmetic, on_device(): bins = binned_t.astype(jnp.bfloat16).reshape(sources, feats, row_count)  1.13 us

profile of v3, /device:TPU:0, one launch (start us, length us, event | category | flops | bytes accessed | tf_op | source)
XLA Modules:
  0.0 40.6 jit_solution(877298261117284506)
XLA Ops:
  0.6 0.0 copy-start
  0.6 0.0 copy-start.1
  0.7 1.1 %convert_element_type.29 = bf16[2048,64]{0,1:T(8,128)(2,1)S(1)} convert(s32[2048,64]{0,1:T(8,128)} %param.6) | non-fusion elementwise | flops 131072 | bytes 786432 | tf_op jit(solution)/shard_map/convert_element_type | solution.py:227
  1.8 0.0 copy-done.1
  1.8 0.0 copy-start.3
  1.8 0.0 copy-start.4
  1.8 0.7 %copy-done.3 = f32[2048]{0:T(1024)S(1)} copy-done((f32[2048]{0:T(1024)S(1)}, f32[2048]{0:T(1024)}, u32[]{:S(2)}) %copy-start.3) | copy-done | bytes 8216
  2.5 0.0 copy-done.4
  2.5 0.0 copy-start.5
  2.5 0.0 copy-start.6
  2.6 0.6 %copy-done.5 = s32[32]{0:T(128)S(1)} copy-done((s32[32]{0:T(128)S(1)}, s32[32]{0:T(128)}, u32[]{:S(2)}) %copy-start.5) | copy-done | bytes 152
  3.2 0.0 copy-done.6
  3.2 0.2 select_reduce_fusion.2
  3.4 0.0 copy-done
  3.4 0.1 convert_reduce_fusion
  3.5 33.7 %shard_map.93 = (bf16[4,16,16,256]{3,2,1,0:T(8,128)(2,1)S(1)}, s32[1,2048]{1,0:T(1,128)S(1)}, f32[32,128]{1,0:T(8,128)S(1)}) custom-call(bf16[4,16,2048]{2,1,0:T(8,128)(2,1)S(1)} %bitcast.15, f32[3,2048]{1,0:T(4,128)S(1)} %pad_maximum_fusion.meta_ref, s32[1,2048]{1,0:T(1,128)S(1)} %bitcast.16), custom_call_target="tpu_custom_call" | custom-call | tf_op jit(solution)/shard_map/pallas_call | solution.py:233
  37.2 0.1 convert_bitcast_fusion
  37.3 1.6 %copy.13 = f32[16,4,16,256]{3,2,1,0:T(8,128)} copy(f32[16,4,16,256]{3,0,2,1:T(8,128)S(1)} %convert_bitcast_fusion) | data formatting | bytes 2097152
  38.9 0.2 fusion.2
  39.1 0.1 select_reduce_fusion
  39.3 0.0 copy-start.2
  39.3 0.6 %multiply_add_fusion = s32[2048]{0:T(1024)} fusion(s32[2048]{0:T(1024)S(1)} %bitcast.17, s32[2048]{0:T(1024)S(1)} %copy-done.1), kind=kLoop, calls=%fused_computation.19 | loop fusion | flops 4096 | bytes 24576 | tf_op jit(solution)/shard_map/add | solution.py:274
  39.9 0.0 copy-done.2
  39.9 0.6 %pad_maximum_fusion.1 = f32[2,2048]{1,0:T(2,128)} fusion(f32[1,2048]{1,0:T(1,128)S(1)} %bitcast.23, f32[1,2048]{1,0:T(1,128)S(1)} %bitcast.20), kind=kLoop, calls=%fused_computation.10 | loop fusion | flops 4096 | bytes 32768 | tf_op jit(solution)/shard_map/stack | solution.py:276
  (7 shorter events, 0.1 us)
Async XLA Ops:
  0.6 2.7 %copy-start = (s32[2048,64]{0,1:T(8,128)S(1)}, s32[2048,64]{0,1:T(8,128)}, u32[]{:S(2)}) copy-start(s32[2048,64]{0,1:T(8,128)} %param.6) | copy-start | bytes 1572868
  0.6 1.1 %copy-start.1 = (s32[2048]{0:T(1024)S(1)}, s32[2048]{0:T(1024)}, u32[]{:S(2)}) copy-start(s32[2048]{0:T(1024)} %param.7) | copy-start | bytes 24580
  1.8 0.7 %copy-start.3 = (f32[2048]{0:T(1024)S(1)}, f32[2048]{0:T(1024)}, u32[]{:S(2)}) copy-start(f32[2048]{0:T(1024)} %param.9) | copy-start | bytes 24580
  1.8 0.7 %copy-start.4 = (f32[2048]{0:T(1024)S(1)}, f32[2048]{0:T(1024)}, u32[]{:S(2)}) copy-start(f32[2048]{0:T(1024)} %param.8) | copy-start | bytes 24580
  2.5 0.7 %copy-start.5 = (s32[32]{0:T(128)S(1)}, s32[32]{0:T(128)}, u32[]{:S(2)}) copy-start(s32[32]{0:T(128)} %param.10) | copy-start | bytes 388
  2.5 0.7 %copy-start.6 = (s32[32]{0:T(128)S(1)}, s32[32]{0:T(128)}, u32[]{:S(2)}) copy-start(s32[32]{0:T(128)} %param.11) | copy-start | bytes 388
  39.3 0.6 %copy-start.2 = (f32[2048]{0:T(1024)}, f32[2048]{0:T(1024)S(1)}, u32[]{:S(2)}) copy-start(f32[2048]{0:T(1024)S(1)} %get-tuple-element.27) | copy-start | bytes 24580

commit v4 on v3

--- a/solution.py
+++ b/solution.py
@@ -27,6 +27,7 @@
     column = lax.axis_index("feat")
     share = 2 * nodes // sources
     groups = feats // GROUP
+    last = range(max(1, sources - 2), sources)
 
     def row_peer(step):
         return lax.rem(me + step, sources)
@@ -47,90 +48,90 @@
         return carry
 
     lax.fori_loop(1, columns, greet, 0)
-    pl.semaphore_wait(barrier, sources - 1 + columns - 1)
-
-    def raw_copy(step, slot, peer):
-        return pltpu.make_async_remote_copy(
-            src_ref=bins_ref.at[peer], dst_ref=raw_in.at[slot],
-            send_sem=raw_send.at[step], recv_sem=raw_recv.at[slot],
-            device_id={"rows": peer}, device_id_type=MESH,
-        )
-
-    def meta_copy(step, slot, peer):
-        return pltpu.make_async_remote_copy(
-            src_ref=meta_ref, dst_ref=meta_in.at[slot],
-            send_sem=meta_send.at[step], recv_sem=meta_recv.at[slot],
-            device_id={"rows": peer}, device_id_type=MESH,
-        )
-
-    def bits_copy(step, slot, peer):
-        return pltpu.make_async_remote_copy(
-            src_ref=bits_ref, dst_ref=bits_in.at[slot],
-            send_sem=bits_send.at[step], recv_sem=bits_recv.at[slot],
-            device_id={"feat": peer}, device_id_type=MESH,
-        )
-
-    def table_copy(step, slot, peer):
-        return pltpu.make_async_remote_copy(
-            src_ref=table_ref, dst_ref=table_in.at[slot],
-            send_sem=table_send.at[step], recv_sem=table_recv.at[slot],
-            device_id={"rows": peer}, device_id_type=MESH,
-        )
-
-    def hist_copy(step, slot, peer, group):
-        part = pl.ds(group * GROUP, GROUP)
-        return pltpu.make_async_remote_copy(
-            src_ref=staged.at[peer, part], dst_ref=hist_ref.at[slot, part],
-            send_sem=hist_send.at[step, group], recv_sem=hist_recv.at[slot, group],
-            device_id={"rows": peer}, device_id_type=MESH,
-        )
-
-    def send_bits(step, carry):
-        bits_copy(step, column, feat_peer(step)).start()
-        return carry
-
-    lax.fori_loop(1, columns, send_bits, 0)
-    for step in range(1, sources):
-        meta_copy(step, me, row_peer(step)).start()
-        raw_copy(step, me, row_peer(step)).start()
-
     bin_ids = lax.broadcasted_iota(jnp.int32, (BINS, row_count), 0).astype(jnp.bfloat16)
     cells = lax.broadcasted_iota(jnp.int32, (2 * nodes, row_count), 0)
     cell_node = cells // 2
     is_grad = cells % 2 == 0
 
-    def set_block(bins, meta):
-        held[...] = bins.astype(jnp.float32)
+    def set_block(step, bins, meta):
+        held[step] = bins.astype(jnp.float32)
         node = meta[2:3].astype(jnp.int32)
         pair = jnp.where(is_grad, meta[0:1], meta[1:2])
         value = jnp.where(cell_node == node, pair * SCALE, 0.0)
         coarse = value.astype(jnp.float8_e4m3fn)
         rest = (value - coarse.astype(jnp.float32)) * FINE
-        weights[: 2 * nodes] = coarse
-        weights[2 * nodes :] = rest.astype(jnp.float8_e4m3fn)
-
-    def piece_of(feat):
-        bins = held[pl.ds(feat, 1), :].astype(jnp.bfloat16)
+        weights[step, : 2 * nodes] = coarse
+        weights[step, 2 * nodes :] = rest.astype(jnp.float8_e4m3fn)
+
+    def piece_of(step, feat):
+        bins = held[step, pl.ds(feat, 1), :].astype(jnp.bfloat16)
         hot = jnp.where(bin_ids == bins, jnp.bfloat16(1), jnp.bfloat16(0))
         hot = hot.astype(jnp.float8_e4m3fn)
         return lax.dot_general(
-            weights[...], hot, (((1,), (1,)), ((), ())), preferred_element_type=jnp.float32
-        )
-
-    def add_block(first):
+            weights[step], hot, (((1,), (1,)), ((), ())), preferred_element_type=jnp.float32
+        )
+
+    def add_block(step):
         def add_pair(index, carry):
             for offset in range(PAIR):
                 feat = index * PAIR + offset
-                if first:
-                    total[feat] = piece_of(feat)
+                if step == 0:
+                    total[feat] = piece_of(step, feat)
                 else:
-                    total[feat] += piece_of(feat)
+                    total[feat] += piece_of(step, feat)
             return carry
 
         lax.fori_loop(0, feats // PAIR, add_pair, 0)
 
-    set_block(bins_ref[me], meta_ref[...])
-    add_block(True)
+    set_block(0, bins_ref[me], meta_ref[...])
+    pl.semaphore_wait(barrier, sources - 1 + columns - 1)
+
+    def raw_copy(step, slot, peer):
+        return pltpu.make_async_remote_copy(
+            src_ref=bins_ref.at[peer], dst_ref=raw_in.at[slot],
+            send_sem=raw_send.at[step], recv_sem=raw_recv.at[slot],
+            device_id={"rows": peer}, device_id_type=MESH,
+        )
+
+    def meta_copy(step, slot, peer):
+        return pltpu.make_async_remote_copy(
+            src_ref=meta_ref, dst_ref=meta_in.at[slot],
+            send_sem=meta_send.at[step], recv_sem=meta_recv.at[slot],
+            device_id={"rows": peer}, device_id_type=MESH,
+        )
+
+    def bits_copy(step, slot, peer):
+        return pltpu.make_async_remote_copy(
+            src_ref=bits_ref, dst_ref=bits_in.at[slot],
+            send_sem=bits_send.at[step], recv_sem=bits_recv.at[slot],
+            device_id={"feat": peer}, device_id_type=MESH,
+        )
+
+    def table_copy(step, slot, peer):
+        return pltpu.make_async_remote_copy(
+            src_ref=table_ref, dst_ref=table_in.at[slot],
+            send_sem=table_send.at[step], recv_sem=table_recv.at[slot],
+            device_id={"rows": peer}, device_id_type=MESH,
+        )
+
+    def hist_copy(step, slot, peer, group):
+        part = pl.ds(group * GROUP, GROUP)
+        return pltpu.make_async_remote_copy(
+            src_ref=staged.at[peer, part], dst_ref=hist_ref.at[slot, part],
+            send_sem=hist_send.at[step, group], recv_sem=hist_recv.at[slot, group],
+            device_id={"rows": peer}, device_id_type=MESH,
+        )
+
+    def send_bits(step, carry):
+        bits_copy(step, column, feat_peer(step)).start()
+        return carry
+
+    lax.fori_loop(1, columns, send_bits, 0)
+    for step in range(1, sources):
+        meta_copy(step, me, row_peer(step)).start()
+        raw_copy(step, me, row_peer(step)).start()
+
+    add_block(0)
 
     go_ref[...] = bits_ref[...]
 
@@ -160,14 +161,16 @@
         peer = row_peer(step)
         meta_copy(step, peer, peer).wait_recv()
         raw_copy(step, peer, peer).wait_recv()
-        set_block(raw_in[peer], meta_in[peer])
-        if step < sources - 1:
-            add_block(False)
+        set_block(step, raw_in[peer], meta_in[peer])
+        if step not in last:
+            add_block(step)
 
     def finish(group, carry):
         for offset in range(GROUP):
             feat = group * GROUP + offset
-            both = total[feat] + piece_of(feat)
+            both = total[feat]
+            for step in last:
+                both += piece_of(step, feat)
             done = both[: 2 * nodes] + both[2 * nodes :] * (1.0 / FINE)
             done = (done * (1.0 / SCALE)).astype(jnp.bfloat16)
             for dest in range(sources):
@@ -213,8 +216,8 @@
     share = 2 * nodes // sources
     feat_start = lax.axis_index("feat") * feat_count
     probability = jax.nn.sigmoid(margin)
-    gradient = (probability - labels).astype(jnp.bfloat16)
-    hessian = (probability * (1.0 - probability)).astype(jnp.bfloat16)
+    gradient = lax.reduce_precision(probability - labels, 8, 7)
+    hessian = lax.reduce_precision(probability * (1.0 - probability), 8, 7)
     node_hot = node_of[None, :] == jnp.arange(nodes, dtype=jnp.int32)[:, None]
     row_feature = jnp.sum(jnp.where(node_hot, split_feature[:, None], 0), axis=0)
     row_cut = jnp.sum(jnp.where(node_hot, split_bin[:, None], 0), axis=0)
@@ -225,9 +228,7 @@
         (column_hot & (binned_t > row_cut[None, :])).astype(jnp.int32), axis=0, keepdims=True
     )
     bins = binned_t.astype(jnp.bfloat16).reshape(sources, feats, row_count)
-    meta = jnp.stack(
-        [gradient.astype(jnp.float32), hessian.astype(jnp.float32), node_of.astype(jnp.float32)]
-    )
+    meta = jnp.stack([gradient, hessian, node_of.astype(jnp.float32)])
     vmem = pl.BlockSpec(memory_space=pltpu.VMEM)
     dma = pltpu.SemaphoreType.DMA
     hist, go_right, table = pl.pallas_call(
@@ -244,8 +245,8 @@
             pltpu.VMEM((sources, 3, row_count), jnp.float32),
             pltpu.VMEM((columns, 1, row_count), jnp.int32),
             pltpu.VMEM((sources, nodes, 128), jnp.float32),
-            pltpu.VMEM((feats, row_count), jnp.float32),
-            pltpu.VMEM((4 * nodes, row_count), jnp.float8_e4m3fn),
+            pltpu.VMEM((sources, feats, row_count), jnp.float32),
+            pltpu.VMEM((sources, 4 * nodes, row_count), jnp.float8_e4m3fn),
             pltpu.VMEM((feats, 4 * nodes, BINS), jnp.float32),
             pltpu.VMEM((sources, feats, share, BINS), jnp.bfloat16),
             dma((sources,)),

time: 40.9 us -> 38.7 us (0.946)
  Pallas kernels: 33.7 us -> 31.5 us
    pallas_call x1, Pallas kernels: 33.7 us -> 31.5 us  [on_device(): pl.pallas_call(functools.partial(level_kernel, sources, columns, nodes, f...]
where the time goes in v4:
time: 38.7 us; the launch traced here: 38.4 us
  Pallas kernels  31.5 us (81%)
  other arithmetic  3.18 us (8%)
  local copies, waits for them, and re-layouts  2.92 us (8%)
  between operations  0.78 us (2%)
    pallas_call x1, Pallas kernels, on_device(): pl.pallas_call(functools.partial(level_kernel, sources, columns, nodes, f...  31.5 us
    unnamed x15, local copies, waits for them, and re-layouts  2.92 us
    convert_element_type x1, other arithmetic, on_device(): bins = binned_t.astype(jnp.bfloat16).reshape(sources, feats, row_count)  1.13 us

profile of v4, /device:TPU:0, one launch (start us, length us, event | category | flops | bytes accessed | tf_op | source)
XLA Modules:
  0.0 38.4 jit_solution(11348532536636657533)
XLA Ops:
  0.6 0.0 copy-start
  0.6 0.0 copy-start.1
  0.7 1.1 %convert_element_type.21 = bf16[2048,64]{0,1:T(8,128)(2,1)S(1)} convert(s32[2048,64]{0,1:T(8,128)} %param.6) | non-fusion elementwise | flops 131072 | bytes 786432 | tf_op jit(solution)/shard_map/convert_element_type | solution.py:230
  1.8 0.0 copy-done.1
  1.8 0.0 copy-start.3
  1.8 0.0 copy-start.4
  1.8 0.7 %copy-done.3 = f32[2048]{0:T(1024)S(1)} copy-done((f32[2048]{0:T(1024)S(1)}, f32[2048]{0:T(1024)}, u32[]{:S(2)}) %copy-start.3) | copy-done | bytes 8216
  2.5 0.0 copy-done.4
  2.5 0.0 copy-start.5
  2.5 0.0 copy-start.6
  2.6 0.6 %copy-done.5 = s32[32]{0:T(128)S(1)} copy-done((s32[32]{0:T(128)S(1)}, s32[32]{0:T(128)}, u32[]{:S(2)}) %copy-start.5) | copy-done | bytes 152
  3.2 0.0 copy-done.6
  3.2 0.2 select_reduce_fusion.2
  3.4 0.0 copy-done
  3.4 0.1 convert_reduce_fusion
  3.5 31.5 %shard_map.93 = (bf16[4,16,16,256]{3,2,1,0:T(8,128)(2,1)S(1)}, s32[1,2048]{1,0:T(1,128)S(1)}, f32[32,128]{1,0:T(8,128)S(1)}) custom-call(bf16[4,16,2048]{2,1,0:T(8,128)(2,1)S(1)} %bitcast.15, f32[3,2048]{1,0:T(4,128)S(1)} %pad_maximum_fusion.meta_ref, s32[1,2048]{1,0:T(1,128)S(1)} %bitcast.16), custom_call_target="tpu_custom_call" | custom-call | tf_op jit(solution)/shard_map/pallas_call | solution.py:234
  35.0 0.1 convert_bitcast_fusion
  35.1 1.6 %copy.13 = f32[16,4,16,256]{3,2,1,0:T(8,128)} copy(f32[16,4,16,256]{3,0,2,1:T(8,128)S(1)} %convert_bitcast_fusion) | data formatting | bytes 2097152
  36.7 0.2 fusion.2
  37.0 0.1 select_reduce_fusion
  37.1 0.0 copy-start.2
  37.1 0.6 %multiply_add_fusion = s32[2048]{0:T(1024)} fusion(s32[2048]{0:T(1024)S(1)} %bitcast.17, s32[2048]{0:T(1024)S(1)} %copy-done.1), kind=kLoop, calls=%fused_computation.19 | loop fusion | flops 4096 | bytes 24576 | tf_op jit(solution)/shard_map/add | solution.py:275
  37.7 0.0 copy-done.2
  37.7 0.6 %pad_maximum_fusion.1 = f32[2,2048]{1,0:T(2,128)} fusion(f32[1,2048]{1,0:T(1,128)S(1)} %bitcast.23, f32[1,2048]{1,0:T(1,128)S(1)} %bitcast.20), kind=kLoop, calls=%fused_computation.10 | loop fusion | flops 4096 | bytes 32768 | tf_op jit(solution)/shard_map/stack | solution.py:277
  (7 shorter events, 0.1 us)
Async XLA Ops:
  0.6 2.7 %copy-start = (s32[2048,64]{0,1:T(8,128)S(1)}, s32[2048,64]{0,1:T(8,128)}, u32[]{:S(2)}) copy-start(s32[2048,64]{0,1:T(8,128)} %param.6) | copy-start | bytes 1572868
  0.6 1.1 %copy-start.1 = (s32[2048]{0:T(1024)S(1)}, s32[2048]{0:T(1024)}, u32[]{:S(2)}) copy-start(s32[2048]{0:T(1024)} %param.7) | copy-start | bytes 24580
  1.8 0.7 %copy-start.3 = (f32[2048]{0:T(1024)S(1)}, f32[2048]{0:T(1024)}, u32[]{:S(2)}) copy-start(f32[2048]{0:T(1024)} %param.9) | copy-start | bytes 24580
  1.8 0.7 %copy-start.4 = (f32[2048]{0:T(1024)S(1)}, f32[2048]{0:T(1024)}, u32[]{:S(2)}) copy-start(f32[2048]{0:T(1024)} %param.8) | copy-start | bytes 24580
  2.5 0.7 %copy-start.5 = (s32[32]{0:T(128)S(1)}, s32[32]{0:T(128)}, u32[]{:S(2)}) copy-start(s32[32]{0:T(128)} %param.10) | copy-start | bytes 388
  2.5 0.7 %copy-start.6 = (s32[32]{0:T(128)S(1)}, s32[32]{0:T(128)}, u32[]{:S(2)}) copy-start(s32[32]{0:T(128)} %param.11) | copy-start | bytes 388
  37.1 0.6 %copy-start.2 = (f32[2048]{0:T(1024)}, f32[2048]{0:T(1024)S(1)}, u32[]{:S(2)}) copy-start(f32[2048]{0:T(1024)S(1)} %get-tuple-element.27) | copy-start | bytes 24580

commit v5 on v4

--- a/solution.py
+++ b/solution.py
@@ -8,7 +8,7 @@
 from jax.sharding import PartitionSpec as P
 
 BINS = 256
-GROUP = 4
+GROUP = 2
 PAIR = 4
 SCALE = 256.0
 FINE = 16.0

time: 38.7 us -> 38.7 us (level)
  no operation moved by 1% of the time
where the time goes in v5:
time: 38.7 us; the launch traced here: 38.4 us
  Pallas kernels  31.6 us (82%)
  other arithmetic  3.18 us (8%)
  local copies, waits for them, and re-layouts  2.92 us (8%)
  between operations  0.78 us (2%)
    pallas_call x1, Pallas kernels, on_device(): pl.pallas_call(functools.partial(level_kernel, sources, columns, nodes, f...  31.6 us
    unnamed x15, local copies, waits for them, and re-layouts  2.92 us
    convert_element_type x1, other arithmetic, on_device(): bins = binned_t.astype(jnp.bfloat16).reshape(sources, feats, row_count)  1.13 us

profile of v5, /device:TPU:0, one launch (start us, length us, event | category | flops | bytes accessed | tf_op | source)
XLA Modules:
  0.0 38.4 jit_solution(4023823014094864469)
XLA Ops:
  0.6 0.0 copy-start
  0.6 0.0 copy-start.1
  0.7 1.1 %convert_element_type.21 = bf16[2048,64]{0,1:T(8,128)(2,1)S(1)} convert(s32[2048,64]{0,1:T(8,128)} %param.6) | non-fusion elementwise | flops 131072 | bytes 786432 | tf_op jit(solution)/shard_map/convert_element_type | solution.py:230
  1.8 0.0 copy-done.1
  1.8 0.0 copy-start.3
  1.8 0.0 copy-start.4
  1.8 0.7 %copy-done.3 = f32[2048]{0:T(1024)S(1)} copy-done((f32[2048]{0:T(1024)S(1)}, f32[2048]{0:T(1024)}, u32[]{:S(2)}) %copy-start.3) | copy-done | bytes 8216
  2.5 0.0 copy-done.4
  2.5 0.0 copy-start.5
  2.5 0.0 copy-start.6
  2.6 0.6 %copy-done.5 = s32[32]{0:T(128)S(1)} copy-done((s32[32]{0:T(128)S(1)}, s32[32]{0:T(128)}, u32[]{:S(2)}) %copy-start.5) | copy-done | bytes 152
  3.2 0.0 copy-done.6
  3.2 0.2 select_reduce_fusion.2
  3.4 0.0 copy-done
  3.4 0.1 convert_reduce_fusion
  3.5 31.6 %shard_map.93 = (bf16[4,16,16,256]{3,2,1,0:T(8,128)(2,1)S(1)}, s32[1,2048]{1,0:T(1,128)S(1)}, f32[32,128]{1,0:T(8,128)S(1)}) custom-call(bf16[4,16,2048]{2,1,0:T(8,128)(2,1)S(1)} %bitcast.15, f32[3,2048]{1,0:T(4,128)S(1)} %pad_maximum_fusion.meta_ref, s32[1,2048]{1,0:T(1,128)S(1)} %bitcast.16), custom_call_target="tpu_custom_call" | custom-call | tf_op jit(solution)/shard_map/pallas_call | solution.py:234
  35.1 0.1 convert_bitcast_fusion
  35.2 1.6 %copy.13 = f32[16,4,16,256]{3,2,1,0:T(8,128)} copy(f32[16,4,16,256]{3,0,2,1:T(8,128)S(1)} %convert_bitcast_fusion) | data formatting | bytes 2097152
  36.8 0.2 fusion.2
  37.0 0.1 select_reduce_fusion
  37.2 0.0 copy-start.2
  37.2 0.6 %multiply_add_fusion = s32[2048]{0:T(1024)} fusion(s32[2048]{0:T(1024)S(1)} %bitcast.17, s32[2048]{0:T(1024)S(1)} %copy-done.1), kind=kLoop, calls=%fused_computation.19 | loop fusion | flops 4096 | bytes 24576 | tf_op jit(solution)/shard_map/add | solution.py:275
  37.8 0.0 copy-done.2
  37.8 0.6 %pad_maximum_fusion.1 = f32[2,2048]{1,0:T(2,128)} fusion(f32[1,2048]{1,0:T(1,128)S(1)} %bitcast.23, f32[1,2048]{1,0:T(1,128)S(1)} %bitcast.20), kind=kLoop, calls=%fused_computation.10 | loop fusion | flops 4096 | bytes 32768 | tf_op jit(solution)/shard_map/stack | solution.py:277
  (7 shorter events, 0.1 us)
Async XLA Ops:
  0.6 2.7 %copy-start = (s32[2048,64]{0,1:T(8,128)S(1)}, s32[2048,64]{0,1:T(8,128)}, u32[]{:S(2)}) copy-start(s32[2048,64]{0,1:T(8,128)} %param.6) | copy-start | bytes 1572868
  0.6 1.1 %copy-start.1 = (s32[2048]{0:T(1024)S(1)}, s32[2048]{0:T(1024)}, u32[]{:S(2)}) copy-start(s32[2048]{0:T(1024)} %param.7) | copy-start | bytes 24580
  1.8 0.7 %copy-start.3 = (f32[2048]{0:T(1024)S(1)}, f32[2048]{0:T(1024)}, u32[]{:S(2)}) copy-start(f32[2048]{0:T(1024)} %param.9) | copy-start | bytes 24580
  1.8 0.7 %copy-start.4 = (f32[2048]{0:T(1024)S(1)}, f32[2048]{0:T(1024)}, u32[]{:S(2)}) copy-start(f32[2048]{0:T(1024)} %param.8) | copy-start | bytes 24580
  2.5 0.7 %copy-start.5 = (s32[32]{0:T(128)S(1)}, s32[32]{0:T(128)}, u32[]{:S(2)}) copy-start(s32[32]{0:T(128)} %param.10) | copy-start | bytes 388
  2.5 0.7 %copy-start.6 = (s32[32]{0:T(128)S(1)}, s32[32]{0:T(128)}, u32[]{:S(2)}) copy-start(s32[32]{0:T(128)} %param.11) | copy-start | bytes 388
  37.2 0.6 %copy-start.2 = (f32[2048]{0:T(1024)}, f32[2048]{0:T(1024)S(1)}, u32[]{:S(2)}) copy-start(f32[2048]{0:T(1024)S(1)} %get-tuple-element.27) | copy-start | bytes 24580

commit v6 on v5

--- a/solution.py
+++ b/solution.py
@@ -126,10 +126,10 @@
         bits_copy(step, column, feat_peer(step)).start()
         return carry
 
-    lax.fori_loop(1, columns, send_bits, 0)
     for step in range(1, sources):
         meta_copy(step, me, row_peer(step)).start()
         raw_copy(step, me, row_peer(step)).start()
+    lax.fori_loop(1, columns, send_bits, 0)
 
     add_block(0)
 

time: 38.7 us -> 38.7 us (level)
  no operation moved by 1% of the time
where the time goes in v6:
time: 38.7 us; the launch traced here: 38.4 us
  Pallas kernels  31.6 us (82%)
  other arithmetic  3.18 us (8%)
  local copies, waits for them, and re-layouts  2.92 us (8%)
  between operations  0.78 us (2%)
    pallas_call x1, Pallas kernels, on_device(): pl.pallas_call(functools.partial(level_kernel, sources, columns, nodes, f...  31.6 us
    unnamed x15, local copies, waits for them, and re-layouts  2.92 us
    convert_element_type x1, other arithmetic, on_device(): bins = binned_t.astype(jnp.bfloat16).reshape(sources, feats, row_count)  1.13 us

profile of v6, /device:TPU:0, one launch (start us, length us, event | category | flops | bytes accessed | tf_op | source)
XLA Modules:
  0.0 38.4 jit_solution(12813062049353162620)
XLA Ops:
  0.6 0.0 copy-start
  0.6 0.0 copy-start.1
  0.7 1.1 %convert_element_type.21 = bf16[2048,64]{0,1:T(8,128)(2,1)S(1)} convert(s32[2048,64]{0,1:T(8,128)} %param.6) | non-fusion elementwise | flops 131072 | bytes 786432 | tf_op jit(solution)/shard_map/convert_element_type | solution.py:230
  1.8 0.0 copy-done.1
  1.8 0.0 copy-start.3
  1.8 0.0 copy-start.4
  1.8 0.7 %copy-done.3 = f32[2048]{0:T(1024)S(1)} copy-done((f32[2048]{0:T(1024)S(1)}, f32[2048]{0:T(1024)}, u32[]{:S(2)}) %copy-start.3) | copy-done | bytes 8216
  2.5 0.0 copy-done.4
  2.5 0.0 copy-start.5
  2.5 0.0 copy-start.6
  2.6 0.6 %copy-done.5 = s32[32]{0:T(128)S(1)} copy-done((s32[32]{0:T(128)S(1)}, s32[32]{0:T(128)}, u32[]{:S(2)}) %copy-start.5) | copy-done | bytes 152
  3.2 0.0 copy-done.6
  3.2 0.2 select_reduce_fusion.2
  3.4 0.0 copy-done
  3.4 0.1 convert_reduce_fusion
  3.5 31.6 %shard_map.93 = (bf16[4,16,16,256]{3,2,1,0:T(8,128)(2,1)S(1)}, s32[1,2048]{1,0:T(1,128)S(1)}, f32[32,128]{1,0:T(8,128)S(1)}) custom-call(bf16[4,16,2048]{2,1,0:T(8,128)(2,1)S(1)} %bitcast.15, f32[3,2048]{1,0:T(4,128)S(1)} %pad_maximum_fusion.meta_ref, s32[1,2048]{1,0:T(1,128)S(1)} %bitcast.16), custom_call_target="tpu_custom_call" | custom-call | tf_op jit(solution)/shard_map/pallas_call | solution.py:234
  35.1 0.1 convert_bitcast_fusion
  35.2 1.6 %copy.13 = f32[16,4,16,256]{3,2,1,0:T(8,128)} copy(f32[16,4,16,256]{3,0,2,1:T(8,128)S(1)} %convert_bitcast_fusion) | data formatting | bytes 2097152
  36.8 0.2 fusion.2
  37.0 0.1 select_reduce_fusion
  37.2 0.0 copy-start.2
  37.2 0.6 %multiply_add_fusion = s32[2048]{0:T(1024)} fusion(s32[2048]{0:T(1024)S(1)} %bitcast.17, s32[2048]{0:T(1024)S(1)} %copy-done.1), kind=kLoop, calls=%fused_computation.19 | loop fusion | flops 4096 | bytes 24576 | tf_op jit(solution)/shard_map/add | solution.py:275
  37.8 0.0 copy-done.2
  37.8 0.6 %pad_maximum_fusion.1 = f32[2,2048]{1,0:T(2,128)} fusion(f32[1,2048]{1,0:T(1,128)S(1)} %bitcast.23, f32[1,2048]{1,0:T(1,128)S(1)} %bitcast.20), kind=kLoop, calls=%fused_computation.10 | loop fusion | flops 4096 | bytes 32768 | tf_op jit(solution)/shard_map/stack | solution.py:277
  (7 shorter events, 0.1 us)
Async XLA Ops:
  0.6 2.7 %copy-start = (s32[2048,64]{0,1:T(8,128)S(1)}, s32[2048,64]{0,1:T(8,128)}, u32[]{:S(2)}) copy-start(s32[2048,64]{0,1:T(8,128)} %param.6) | copy-start | bytes 1572868
  0.6 1.1 %copy-start.1 = (s32[2048]{0:T(1024)S(1)}, s32[2048]{0:T(1024)}, u32[]{:S(2)}) copy-start(s32[2048]{0:T(1024)} %param.7) | copy-start | bytes 24580
  1.8 0.7 %copy-start.3 = (f32[2048]{0:T(1024)S(1)}, f32[2048]{0:T(1024)}, u32[]{:S(2)}) copy-start(f32[2048]{0:T(1024)} %param.9) | copy-start | bytes 24580
  1.8 0.7 %copy-start.4 = (f32[2048]{0:T(1024)S(1)}, f32[2048]{0:T(1024)}, u32[]{:S(2)}) copy-start(f32[2048]{0:T(1024)} %param.8) | copy-start | bytes 24580
  2.5 0.7 %copy-start.5 = (s32[32]{0:T(128)S(1)}, s32[32]{0:T(128)}, u32[]{:S(2)}) copy-start(s32[32]{0:T(128)} %param.10) | copy-start | bytes 388
  2.5 0.7 %copy-start.6 = (s32[32]{0:T(128)S(1)}, s32[32]{0:T(128)}, u32[]{:S(2)}) copy-start(s32[32]{0:T(128)} %param.11) | copy-start | bytes 388
  37.2 0.6 %copy-start.2 = (f32[2048]{0:T(1024)}, f32[2048]{0:T(1024)S(1)}, u32[]{:S(2)}) copy-start(f32[2048]{0:T(1024)S(1)} %get-tuple-element.27) | copy-start | bytes 24580
